TPU v7x, 32 devices: a whole 2x2x4 slice. The times are simulated.
32 devices in a mesh: groups: 2 (over y), blk: 4 (over z), red: 2 (over x), sub: 2 (over core).
Axes of the slice: x: 2, y: 2, z: 4, core: 2. Of those that a mesh axis runs over, the one named last changes fastest.
Arguments:
- activations: bfloat16 [2, 16, 128, 8192], P('red', ('groups', 'blk', 'sub')), parts along dimension 1, may hold values from -6 to 6
- out_grads: bfloat16 [2, 16, 128, 8192], P('red', ('groups', 'blk', 'sub')), parts along dimension 1, may hold values from -6 to 6
- lengths: int32 [2, 16], P('red', ('groups', 'blk', 'sub')), parts along dimension 1, may hold values from 32 to 128
- proj_in: bfloat16 [8192, 256], P(('blk', 'red', 'sub')), may hold values from -0.0625 to 0.0625
- proj_out: bfloat16 [8192, 256], P(('blk', 'red', 'sub')), may hold values from -0.0625 to 0.0625
- queries: bfloat16 [512, 256, 256], P(('groups', 'red'), ('blk', 'sub')), parts along dimension 0, may hold values from -6 to 6
Outputs:
- scores: float32 [512, 16], P(('groups', 'blk', 'sub'), 'red'), parts along dimension 0
There are 2 independent parts, one for each index of `groups`. A program takes and returns all parts, laid end to end along the dimension named above; an argument that names none is the same for every part. Nothing has to cross between parts.
All inputs are finite; a program needn't handle non-finite values.
Results may differ from a plain program's by a relative error of at most 0.0051.
Values may be sent and summed in bfloat16 or wider, within the bound.
A program may use at most 128 MiB of HBM per device.

v0:
```python
import math

import jax
import jax.numpy as jnp
from jax import lax
from jax.sharding import PartitionSpec as P

BS = 512
NS_STEPS = 2
BLOCKS = 128


DAMPING = 0.1
HIGH = lax.Precision.HIGHEST


def block_inverse(gram, member, held_blocks):
    size = gram.shape[0]
    ident = jnp.eye(size, dtype=jnp.float32)
    trace = jnp.sum(gram * ident, axis=1, keepdims=True)
    square = jnp.sum(gram * gram, axis=1, keepdims=True)
    trace = jnp.sum(jnp.where(member, trace, 0.0), axis=0, keepdims=True)
    square = jnp.sum(jnp.where(member, square, 0.0), axis=0, keepdims=True)
    damping = DAMPING * trace / BS
    hessian = gram + damping * ident
    scale = lax.rsqrt(square + 2.0 * damping * trace + BS * damping * damping)
    inverse = scale * (2.0 * ident - scale * hessian)
    for sweep in range(NS_STEPS):
        image = jnp.dot(hessian, inverse, precision=HIGH)
        inverse = jnp.dot(inverse, 2.0 * ident - image, precision=HIGH)
    return inverse


def on_device(activations, out_grads, lengths, proj_in, proj_out, queries):
    ex_dev = activations.shape[1]
    seq_len = activations.shape[2]
    model_width = activations.shape[3]
    rank_in = proj_in.shape[1]
    rank_out = proj_out.shape[1]
    positions = lax.broadcasted_iota(jnp.int32, (ex_dev, seq_len), 1)
    live_mask = positions < lengths
    tok_rows = activations.reshape(ex_dev * seq_len, model_width)
    masked = jnp.where(
        live_mask.reshape(ex_dev * seq_len, 1),
        out_grads.reshape(ex_dev * seq_len, model_width),
        jnp.zeros((), out_grads.dtype),
    )
    first_sum = jnp.dot(
        tok_rows,
        lax.all_gather(proj_in, ("blk", "red", "sub"), axis=0, tiled=True),
        preferred_element_type=jnp.float32,
    )
    second_sum = jnp.dot(
        masked,
        lax.all_gather(proj_out, ("blk", "red", "sub"), axis=0, tiled=True),
        preferred_element_type=jnp.float32,
    )
    in_side = first_sum
    out_side = second_sum
    in_side = in_side.astype(jnp.bfloat16).reshape(ex_dev, seq_len, rank_in)
    out_side = out_side.astype(jnp.bfloat16).reshape(ex_dev, seq_len, rank_out)
    projected = jnp.einsum(
        "elo,eli->eoi", out_side, in_side, preferred_element_type=jnp.float32
    ).astype(jnp.bfloat16)
    regrouped = lax.all_to_all(projected, ("blk", "sub"), split_axis=1, concat_axis=0, tiled=True)
    held = regrouped.shape[0]
    coords = regrouped.reshape(held, -1, BS)
    every_coord = lax.all_gather(coords, "red", axis=0, tiled=True)
    total_ex, held_blocks = every_coord.shape[:2]
    by_block = every_coord.transpose(1, 0, 2)
    rows = by_block.reshape(held_blocks * total_ex, BS)
    own = jnp.arange(held_blocks * total_ex) // total_ex
    member = own[:, None] == own[None, :]
    gram = jnp.dot(rows, rows.T, preferred_element_type=jnp.float32)
    gram = jnp.where(member, gram, 0.0) / total_ex
    inverse = block_inverse(gram, member, held_blocks)
    query_coords = queries.reshape(queries.shape[0], -1, BS)
    raw = jnp.einsum("qkd,ked->qke", query_coords, by_block, preferred_element_type=jnp.float32)
    raw = raw.reshape(raw.shape[0], -1)
    fold = jnp.sum(inverse.reshape(-1, held_blocks, total_ex), axis=1)
    partial_scores = jnp.dot(raw, fold, precision=HIGH)
    every_score = lax.all_gather(partial_scores, "red", axis=0, tiled=True)
    scores = lax.psum_scatter(every_score, ("blk", "sub"), scatter_dimension=0, tiled=True)
    here = lax.axis_index("red") * held
    scores = lax.dynamic_slice_in_dim(scores, here, held, axis=1)
    return scores * (1.0 / math.sqrt(BLOCKS))


def solution(mesh):
    placed = (
        P("red", ("groups", "blk", "sub"), None, None),
        P("red", ("groups", "blk", "sub"), None, None),
        P("red", ("groups", "blk", "sub")),
        P(("blk", "red", "sub"), None),
        P(("blk", "red", "sub"), None),
        P(("groups", "red"), ("blk", "sub"), None),
    )
    return jax.shard_map(
        on_device,
        mesh=mesh,
        in_specs=placed,
        out_specs=P(("groups", "blk", "sub"), "red"),
        check_vma=False,
    )
```

profile of v0, /device:TPU:0, one launch (start us, length us, event | category | flops | bytes accessed | tf_op | source)
XLA Modules:
  0.0 182.8 jit_solution(10226351170530702439)
XLA Ops:
  6.5 0.7 all-gather.3.cloned.1.call-update
  7.3 0.7 all-gather.5.cloned.1.call-update
  8.7 54.2 %all-gather.3.cloned.1.call-done = bf16[8192,256]{1,0:T(8,128)(2,1)} async-done(((bf16[512,256]{1,0:T(8,128)(2,1)}), bf16[8192,256]{1,0:T(8,128)(2,1)}) %all-gather.3.cloned.1.call-update) | async-done | bytes 4194320 | tf_op jit(solution)/shard_map/all_gather | solution.py:55
  62.8 3.6 %fusion.8 = bf16[128,256]{1,0:T(8,128)(2,1)S(1)} fusion(bf16[8192,256]{1,0:T(8,128)(2,1)} %all-gather.3.cloned.1.call-done, bf16[1,1,128,8192]{3,2,1,0:T(8,128)(2,1)} %param.7, pred[128]{0:T(512)(128)(4,1)S(1)} %iota_compare_fusion.3), kind=kOutput, calls=%fused_computation.13 | convolution fusion | flops 537952256 | bytes 6357120 | tf_op jit(solution)/shard_map/dot_general | solution.py:53
  66.4 47.7 %all-gather.5.cloned.1.call-done = bf16[8192,256]{1,0:T(8,128)(2,1)} async-done(((bf16[512,256]{1,0:T(8,128)(2,1)}), bf16[8192,256]{1,0:T(8,128)(2,1)}) %all-gather.5.cloned.1.call-update) | async-done | bytes 4194320 | tf_op jit(solution)/shard_map/all_gather | solution.py:50
  114.1 3.1 %fusion.7 = bf16[1,256,256]{2,1,0:T(8,128)(2,1)S(1)} fusion(bf16[128,256]{1,0:T(8,128)(2,1)S(1)} %fusion.8, bf16[8192,256]{1,0:T(8,128)(2,1)} %all-gather.5.cloned.1.call-done, bf16[1,1,128,8192]{3,2,1,0:T(8,128)(2,1)S(1)} %copy-done), kind=kOutput, calls=%fused_computation.12 | convolution fusion | flops 553746432 | bytes 6488064 | tf_op jit(solution)/shard_map/elo,eli->eoi/dot_general | solution.py:62
  117.4 0.5 broadcast.106
  117.9 1.4 reduce.2
  119.3 0.7 reshape.103
  120.0 3.4 %all-to-all-start = ((bf16[8,2,4096]{2,1,0:T(2,128)(2,1)}), bf16[8,2,4096]{2,1,0:T(2,128)(2,1)S(1)}, u32[]{:S(2)}, u32[]{:S(2)}) async-start(bf16[8,2,4096]{2,1,0:T(2,128)(2,1)} %reshape.103), calls=%async_computation | async-start | bytes 262144 | tf_op jit(solution)/shard_map/all_to_all | solution.py:65
  123.4 4.1 %reshape.96 = bf16[128,16,512]{2,1,0:T(8,128)(2,1)} reshape(bf16[128,32,256]{2,1,0:T(8,128)(2,1)} %param.11) | data formatting | bytes 4194304 | tf_op jit(solution)/shard_map/reshape | solution.py:77
  127.5 2.6 %all-to-all-done = bf16[8,2,4096]{2,1,0:T(2,128)(2,1)S(1)} async-done(((bf16[8,2,4096]{2,1,0:T(2,128)(2,1)}), bf16[8,2,4096]{2,1,0:T(2,128)(2,1)S(1)}, u32[]{:S(2)}, u32[]{:S(2)}) %all-to-all-start) | async-done | bytes 131104 | tf_op jit(solution)/shard_map/all_to_all | solution.py:65
  130.2 0.7 bitcast_reduce_fusion
  131.1 5.6 %all_gather.14 = bf16[16,16,512]{2,0,1:T(8,128)(2,1)S(1)} all-gather(bf16[8,16,512]{2,0,1:T(8,128)(2,1)S(1)} %copy.12), channel_id=1, replica_groups=mesh['groups'=2,'blk'=4,'red'=2,'sub'=2] {'red'}, dimensions={0}, use_global_device_ids=true | all-gather | bytes 393216 | tf_op jit(solution)/shard_map/all_gather | solution.py:68
  137.3 0.5 convolution_subtract_fusion.1
  137.8 0.7 fusion.19
  138.5 0.7 convolution_subtract_fusion
  139.1 0.4 fusion.41
  139.6 1.2 fusion.3
  141.0 4.4 %all_gather.15 = f32[256,16]{0,1:T(8,128)S(1)} all-gather(f32[128,16]{0,1:T(8,128)S(1)} %fusion.42), channel_id=1, replica_groups=mesh['groups'=2,'blk'=4,'red'=2,'sub'=2] {'red'}, dimensions={0}, use_global_device_ids=true | all-gather | bytes 24576 | tf_op jit(solution)/shard_map/all_gather | solution.py:82
  145.4 0.7 copy.18
  146.1 28.7 %reduce-scatter.4.cloned.1.call-done = f32[32,16]{1,0:T(8,128)} async-done(((f32[256,16]{1,0:T(8,128)}), f32[32,16]{1,0:T(8,128)}) %reduce-scatter.4.cloned.1.call-update) | async-done | bytes 2064
  174.8 0.8 constant_dynamic-slice_fusion
  175.7 0.6 broadcast_multiply_fusion
  (20 shorter events, 1.4 us)
Async XLA Ops:
  6.5 107.5 %copy-start = (bf16[1,1,128,8192]{3,2,1,0:T(8,128)(2,1)S(1)}, bf16[1,1,128,8192]{3,2,1,0:T(8,128)(2,1)}, u32[]{:S(2)}) copy-start(bf16[1,1,128,8192]{3,2,1,0:T(8,128)(2,1)} %param.6) | copy-start | bytes 6291460
  6.5 56.3 %all-gather.3.cloned.1.call-start = ((), (), s32[]{:S(2)}) async-start(), calls=%async_computation.2 | async-start | bytes 4456448 | tf_op jit(solution)/shard_map/all_gather | solution.py:55
  7.3 106.8 %all-gather.5.cloned.1.call-start = ((), (), s32[]{:S(2)}) async-start(), calls=%async_computation.3 | async-start | bytes 4456448 | tf_op jit(solution)/shard_map/all_gather | solution.py:50
  120.0 10.1 %all-to-all-start = ((bf16[8,2,4096]{2,1,0:T(2,128)(2,1)}), bf16[8,2,4096]{2,1,0:T(2,128)(2,1)S(1)}, u32[]{:S(2)}, u32[]{:S(2)}) async-start(bf16[8,2,4096]{2,1,0:T(2,128)(2,1)} %reshape.103), calls=%async_computation | async-start | bytes 262144 | tf_op jit(solution)/shard_map/all_to_all | solution.py:65
  123.4 51.4 %reduce-scatter.4.cloned.1.call-start = ((), (), s32[]{:S(2)}) async-start(), calls=%async_computation.4 | async-start | bytes 147456
  136.8 2.8 %copy-start.1 = (bf16[128,16,512]{2,1,0:T(8,128)(2,1)S(1)}, bf16[128,16,512]{2,1,0:T(8,128)(2,1)}, u32[]{:S(2)}) copy-start(bf16[128,16,512]{2,1,0:T(8,128)(2,1)} %reshape.96) | copy-start | bytes 6291460
Sparse Core Ops, SparseCore 0:
  9.5 53.2 all-gather.2
  65.0 49.0 all-gather.4
  146.2 28.5 reduce-scatter.3
where the time goes:
time: 183 us
  waiting for transfers between devices  135 us (74%)
  between operations  13.9 us (8%)
  matrix products  10.6 us (6%)
  blocking collectives  10 us (5%)
  local copies, waits for them, and re-layouts  8.07 us (4%)
  starting transfers between devices  3.45 us (2%)
  other arithmetic  2.28 us (1%)
    all_gather x1, waiting for transfers between devices, on_device(): lax.all_gather(proj_out, ('blk', 'red', 'sub'), axis=0, tiled=True)  54.2 us
    all_gather x1, waiting for transfers between devices, on_device(): lax.all_gather(proj_in, ('blk', 'red', 'sub'), axis=0, tiled=True)  47.7 us
    unnamed x4, waiting for transfers between devices  30.1 us
    all_gather x1, blocking collectives, on_device(): every_coord = lax.all_gather(coords, 'red', axis=0, tiled=True)  5.64 us
    all_gather x1, blocking collectives, on_device(): every_score = lax.all_gather(partial_scores, 'red', axis=0, tiled=True)  4.36 us
    reshape x1, local copies, waits for them, and re-layouts, on_device(): query_coords = queries.reshape(queries.shape[0], -1, BS)  4.07 us
  transfers between devices with their start and end apart: 4, of which 4 were waited for; matrix products, arithmetic and copies ran while one was open for 4% of the time, Pallas kernels for 0%

commit v1 on v0

--- a/solution.py
+++ b/solution.py
@@ -1,8 +1,11 @@
+import functools
 import math
 
 import jax
 import jax.numpy as jnp
 from jax import lax
+from jax.experimental import pallas as pl
+from jax.experimental.pallas import tpu as pltpu
 from jax.sharding import PartitionSpec as P
 
 BS = 512
@@ -86,6 +89,314 @@
     return scores * (1.0 / math.sqrt(BLOCKS))
 
 
+UP, DOWN, ACROSS, OVER, CORE = range(5)
+
+
+def fused(nz, split, a_hbm, g_hbm, len_ref, pin_hbm, pout_hbm, q_hbm, out_ref, pbuf, abuf, gbuf, qbuf, qt, acc,
+          pieces, coords, parts, rbuf, lsem, ssem, rsem, asem_s, asem_r, xsem_s, xsem_r, fsem_s, fsem_r):
+    y, z, x, c = (lax.axis_index(name) for name in ("groups", "blk", "red", "sub"))
+    rows, rank = pbuf.shape[2:]
+    n_tok = abuf.shape[0]
+    n_chunk = nz * 2
+    me = z * 2 + c
+
+    def slot(zz, xx, cc):
+        return (zz * 2 + xx) * 2 + cc
+
+    def remote(src, dst, send, recv, **device):
+        return pltpu.make_async_remote_copy(
+            src_ref=src, dst_ref=dst, send_sem=send, recv_sem=recv,
+            device_id=device, device_id_type=pl.DeviceIdType.MESH)
+
+    own = slot(z, x, c)
+    local = [
+        pltpu.make_async_copy(pin_hbm, pbuf.at[own, 0], lsem.at[0]),
+        pltpu.make_async_copy(pout_hbm, pbuf.at[own, 1], lsem.at[1]),
+        pltpu.make_async_copy(q_hbm, qbuf, lsem.at[2]),
+        pltpu.make_async_copy(a_hbm, abuf, lsem.at[3]),
+        pltpu.make_async_copy(g_hbm, gbuf, lsem.at[4]),
+    ]
+    for item in local:
+        item.start()
+
+    barrier = pltpu.get_barrier_semaphore()
+    greeted = 0
+    for dx in range(2):
+        for step in range(n_chunk):
+            if dx == 0 and step == 0:
+                continue
+            other = lax.rem(me + step, n_chunk)
+            pl.semaphore_signal(barrier, inc=1, device_id={"blk": other // 2, "red": lax.rem(x + dx, 2), "sub": lax.rem(other, 2)},
+                                device_id_type=pl.DeviceIdType.MESH)
+            greeted += 1
+    pl.semaphore_signal(barrier, inc=1, device_id={"groups": 1 - y}, device_id_type=pl.DeviceIdType.MESH)
+    pl.semaphore_wait(barrier, greeted + 1)
+
+    pending = []
+
+    def part(p, at):
+        if isinstance(p, int):
+            return pbuf.at[at, :, pl.ds(split, rows - split), :]
+        return pbuf.at[at, p, pl.ds(0, split), :]
+
+    targets = {UP: lambda: {"blk": lax.min(z + 1, nz - 1)}, DOWN: lambda: {"blk": lax.max(z - 1, 0)},
+               ACROSS: lambda: {"red": 1 - x}, OVER: lambda: {"groups": 1 - y}, CORE: lambda: {"sub": 1 - c}}
+
+    def moved(way, p, at):
+        return remote(part(p, at), part(p, at), ssem.at[way, p, at], rsem.at[p, at], **targets[way]())
+
+    def send(way, p, at, when=None):
+        if when is None:
+            moved(way, p, at).start()
+        else:
+            pl.when(when)(lambda: moved(way, p, at).start())
+        pending.append((way, p, at, when))
+
+    def arrived(p, at):
+        moved(CORE, p, at).wait_recv()
+
+    def multiply(at, first=False):
+        columns = pl.ds(pl.multiple_of(at * rows, rows), rows)
+        for side, tokens in enumerate((abuf, gbuf)):
+            term = jnp.dot(tokens[:, columns], pbuf[at, side], preferred_element_type=jnp.float32)
+            acc[side] = term if first else acc[side] + term
+
+    turns = [sorted(range(nz), key=lambda other: (abs(other - here), other)) for here in range(nz)]
+
+    def turn(k):
+        return sum(jnp.where(z == here, turns[here][k], 0) for here in range(nz)).astype(jnp.int32)
+
+    local[0].wait()
+    local[1].wait()
+    for p in (y, 2):
+        send(UP, p, own, z < nz - 1)
+        send(DOWN, p, own, z > 0)
+        send(ACROSS, p, own)
+    for p in (y, 1 - y, 2):
+        send(CORE, p, own)
+
+    local[2].wait()
+    hh, kb = qt.shape[0], qt.shape[1]
+    step_q = 16
+
+    def regroup(i, carry):
+        at = pl.ds(pl.multiple_of(i * step_q, step_q), step_q)
+        block = jnp.swapaxes(qbuf[at].astype(jnp.float32), 0, 1).astype(jnp.bfloat16)
+        block = block.reshape(kb, hh, step_q, rank)
+        for h in range(hh):
+            qt[h, :, at, :] = block[:, h]
+        return carry
+
+    lax.fori_loop(0, qbuf.shape[0] // step_q, regroup, 0)
+    local[3].wait()
+    local[4].wait()
+    multiply(own, True)
+
+    waiting, twin = [], [slot(z, x, 1 - c)]
+    for k in range(1, nz + 2):
+        fresh = []
+        if k < nz:
+            zk = turn(k)
+            at = slot(zk, x, c)
+            for p in (y, 2):
+                arrived(p, at)
+                send(UP, p, at, jnp.logical_and(zk < z, z < nz - 1))
+                send(DOWN, p, at, jnp.logical_and(zk > z, z > 0))
+                send(ACROSS, p, at)
+                if not isinstance(p, int):
+                    send(OVER, p, at)
+                send(CORE, p, at)
+            fresh.append((zk, x))
+        if k <= nz:
+            zk = turn(k - 1)
+            at = slot(zk, 1 - x, c)
+            for p in (y, 2):
+                arrived(p, at)
+                if not isinstance(p, int):
+                    send(OVER, p, at)
+                send(CORE, p, at)
+            fresh.append((zk, 1 - x))
+        for zk, xk in waiting:
+            at = slot(zk, xk, c)
+            arrived(1 - y, at)
+            send(CORE, 1 - y, at)
+        for at in twin:
+            for p in (y, 1 - y, 2):
+                arrived(p, at)
+            multiply(at)
+        for zk, xk in waiting:
+            multiply(slot(zk, xk, c))
+        twin = [slot(zk, xk, 1 - c) for zk, xk in waiting]
+        waiting = fresh
+    for at in twin:
+        for p in (y, 1 - y, 2):
+            arrived(p, at)
+        multiply(at)
+
+    chunk_rows = hh * kb
+    old = lax.broadcasted_iota(jnp.int32, (rank, rank), 0)
+    new = lax.broadcasted_iota(jnp.int32, (rank, rank), 1)
+    inside = jnp.bitwise_and(new, chunk_rows - 1)
+    source = new - inside + jnp.bitwise_and(inside, kb - 1) * hh + lax.shift_right_logical(inside, kb.bit_length() - 1)
+    order = jnp.where(old == source, 1.0, 0.0).astype(jnp.bfloat16)
+    in_side = acc[0].astype(jnp.bfloat16)
+    live = lax.broadcasted_iota(jnp.int32, (n_tok, rank), 0) < len_ref[0, 0]
+    out_side = jnp.where(live, acc[1], 0.0).astype(jnp.bfloat16)
+    out_side = jnp.dot(out_side, order, preferred_element_type=jnp.float32).astype(jnp.bfloat16)
+    projected = lax.dot_general(out_side, in_side, (((0,), (0,)), ((), ())), preferred_element_type=jnp.float32)
+    pieces[...] = projected.astype(jnp.bfloat16).reshape(pieces.shape)
+
+    def chunk_out(to):
+        return remote(pieces.at[to], coords.at[x * n_chunk + me], asem_s.at[to], asem_r.at[me], blk=to // 2, sub=lax.rem(to, 2))
+
+    def chunk_in(frm):
+        return remote(pieces.at[frm], coords.at[x * n_chunk + frm], asem_s.at[frm], asem_r.at[frm], sub=1 - c)
+
+    def across(of, side):
+        return remote(coords.at[side * n_chunk + of], coords.at[side * n_chunk + of], xsem_s.at[of], xsem_r.at[of], red=1 - x)
+
+    for step in range(1, n_chunk):
+        chunk_out(lax.rem(me + step, n_chunk)).start()
+    coords[x * n_chunk + me] = pieces[me]
+    across(me, x).start()
+    for step in [1, 7, 2, 6, 3, 5, 4] if n_chunk == 8 else range(1, n_chunk):
+        frm = lax.rem(me + step, n_chunk)
+        chunk_in(frm).wait_recv()
+        across(frm, x).start()
+    for of in range(n_chunk):
+        across(of, 1 - x).wait_recv()
+
+    n_ex = coords.shape[0]
+    size = n_ex * kb
+    halves = [coords[:, h].reshape(size, rank) for h in range(hh)]
+    row = lax.broadcasted_iota(jnp.int32, (size, size), 0)
+    col = lax.broadcasted_iota(jnp.int32, (size, size), 1)
+    member = jnp.bitwise_and(row, kb - 1) == jnp.bitwise_and(col, kb - 1)
+    contract = (((1,), (1,)), ((), ()))
+    gram = sum(lax.dot_general(half, half, contract, preferred_element_type=jnp.float32) for half in halves)
+    gram = jnp.where(member, gram, 0.0) / n_ex
+    ident = jnp.where(row == col, 1.0, 0.0)
+    trace = jnp.sum(gram * ident, axis=1, keepdims=True)
+    square = jnp.sum(gram * gram, axis=1, keepdims=True)
+    trace = jnp.sum(jnp.where(member, trace, 0.0), axis=0, keepdims=True)
+    square = jnp.sum(jnp.where(member, square, 0.0), axis=0, keepdims=True)
+    damping = DAMPING * trace / BS
+    hessian = gram + damping * ident
+    scale = lax.rsqrt(square + 2.0 * damping * trace + BS * damping * damping)
+    inverse = scale * (2.0 * ident - scale * hessian)
+
+    n_q = qt.shape[2]
+    lane = jnp.bitwise_and(lax.broadcasted_iota(jnp.int32, (n_q, size), 1), kb - 1)
+    flipped = [half.T for half in halves]
+    raw = jnp.zeros((n_q, size), jnp.float32)
+    for k in range(kb):
+        term = sum(jnp.dot(qt[h, k], flipped[h], preferred_element_type=jnp.float32) for h in range(hh))
+        raw = jnp.where(lane == k, term, raw)
+
+    for sweep in range(NS_STEPS):
+        image = jnp.dot(hessian, inverse, precision=HIGH, preferred_element_type=jnp.float32)
+        rest = 2.0 * ident - image
+        if sweep < NS_STEPS - 1:
+            inverse = jnp.dot(inverse, rest, precision=HIGH, preferred_element_type=jnp.float32)
+    raw = jnp.dot(raw, inverse, precision=HIGH, preferred_element_type=jnp.float32)
+    raw = jnp.dot(raw, rest, precision=HIGH, preferred_element_type=jnp.float32)
+    ex = lax.broadcasted_iota(jnp.int32, (n_ex, size), 0)
+    of_ex = lax.shift_right_logical(lax.broadcasted_iota(jnp.int32, (n_ex, size), 1), kb.bit_length() - 1)
+    fold = jnp.where(ex == of_ex, 1.0, 0.0)
+    total = lax.dot_general(fold, raw, contract, precision=HIGH, preferred_element_type=jnp.float32)
+    parts[...] = total.reshape(parts.shape)
+
+    takers = n_chunk // 2
+
+    def score_out(xx, t):
+        to = takers * x + t
+        return remote(parts.at[xx], rbuf.at[me], fsem_s.at[xx * takers + t], fsem_r.at[me],
+                      blk=to // 2, red=jnp.int32(xx), sub=lax.rem(to, 2))
+
+    def is_self(xx, t):
+        return jnp.logical_and(takers * x + t == me, x == xx)
+
+    for xx in range(2):
+        for t in range(takers):
+            pl.when(jnp.logical_not(is_self(xx, t)))(lambda: score_out(xx, t).start())
+    giver = me // takers
+
+    @pl.when(giver == x)
+    def _():
+        rbuf[me] = parts[x]
+
+    for frm in range(n_chunk):
+        landing = remote(parts.at[0], rbuf.at[frm], fsem_s.at[0], fsem_r.at[frm], sub=1 - c)
+        pl.when(jnp.logical_not(jnp.logical_and(giver == x, me == frm)))(landing.wait_recv)
+    out_ref[...] = jnp.sum(rbuf[...], axis=0)
+
+    for xx in range(2):
+        for t in range(takers):
+            pl.when(jnp.logical_not(is_self(xx, t)))(lambda: score_out(xx, t).wait_send())
+    for step in range(1, n_chunk):
+        chunk_out(lax.rem(me + step, n_chunk)).wait_send()
+    for of in range(n_chunk):
+        across(of, x).wait_send()
+    for way, p, at, when in pending:
+        if when is None:
+            moved(way, p, at).wait_send()
+        else:
+            pl.when(when)(lambda: moved(way, p, at).wait_send())
+
+
+def on_device_fused(activations, out_grads, lengths, proj_in, proj_out, queries):
+    nz = lax.axis_size("blk")
+    seq_len, width = activations.shape[2:]
+    rows, rank = proj_in.shape
+    n_q, held_rows, _ = queries.shape
+    hh = BS // rank
+    kb = held_rows // hh
+    n_chunk = nz * 2
+    n_ex = n_chunk * 2
+    split = rows * 11 // 16
+    anywhere = pl.BlockSpec(memory_space=pl.ANY)
+    dma = pltpu.SemaphoreType.DMA
+    flops = 4 * seq_len * width * rank
+    total = pl.pallas_call(
+        functools.partial(fused, nz, split),
+        out_shape=jax.ShapeDtypeStruct((n_chunk, n_q), jnp.float32),
+        in_specs=[anywhere, anywhere, pl.BlockSpec(memory_space=pltpu.SMEM), anywhere, anywhere, anywhere],
+        out_specs=pl.BlockSpec(memory_space=pltpu.VMEM),
+        scratch_shapes=[
+            pltpu.VMEM((n_chunk * 2, 2, rows, rank), jnp.bfloat16),
+            pltpu.VMEM((seq_len, width), jnp.bfloat16),
+            pltpu.VMEM((seq_len, width), jnp.bfloat16),
+            pltpu.VMEM(queries.shape, jnp.bfloat16),
+            pltpu.VMEM((hh, kb, n_q, rank), jnp.bfloat16),
+            pltpu.VMEM((2, seq_len, rank), jnp.float32),
+            pltpu.VMEM((n_chunk, hh, kb, rank), jnp.bfloat16),
+            pltpu.VMEM((n_ex, hh, kb, rank), jnp.bfloat16),
+            pltpu.VMEM((2, n_chunk, n_q), jnp.float32),
+            pltpu.VMEM((n_chunk, n_chunk, n_q), jnp.float32),
+            dma((5,)),
+            dma((5, 3, n_chunk * 2)),
+            dma((3, n_chunk * 2)),
+            dma((n_chunk,)),
+            dma((n_chunk,)),
+            dma((n_chunk,)),
+            dma((n_chunk,)),
+            dma((n_chunk,)),
+            dma((n_chunk,)),
+        ],
+        compiler_params=pltpu.CompilerParams(collective_id=0, has_side_effects=True, vmem_limit_bytes=48 * 2**20),
+        cost_estimate=pl.CostEstimate(flops=flops, bytes_accessed=7 * 2**20, transcendentals=0),
+    )(activations.reshape(seq_len, width), out_grads.reshape(seq_len, width), lengths, proj_in, proj_out, queries)
+    n_out = n_q * 2 // n_chunk
+    me = lax.axis_index("blk") * 2 + lax.axis_index("sub")
+    mine = lax.dynamic_slice_in_dim(total, lax.rem(me, n_chunk // 2) * n_out, n_out, axis=1)
+    return mine.T * (1.0 / math.sqrt(BLOCKS))
+
+
+def fits(mesh):
+    shape = mesh.shape
+    return shape["groups"] == 2 and shape["red"] == 2 and shape["sub"] == 2 and shape["blk"] == 4
+
+
 def solution(mesh):
     placed = (
         P("red", ("groups", "blk", "sub"), None, None),
@@ -96,7 +407,7 @@
         P(("groups", "red"), ("blk", "sub"), None),
     )
     return jax.shard_map(
-        on_device,
+        on_device_fused if fits(mesh) else on_device,
         mesh=mesh,
         in_specs=placed,
         out_specs=P(("groups", "blk", "sub"), "red"),

time: 183 us -> 69.7 us (0.38)
  waiting for transfers between devices: 135 us -> 0 us
  Pallas kernels: 0 us -> 63 us
  between operations: 13.9 us -> 0.67 us
  matrix products: 10.6 us -> 0 us
  blocking collectives: 10 us -> 0 us
  starting transfers between devices: 3.45 us -> 0 us
  local copies, waits for them, and re-layouts: 8.07 us -> 5.07 us
    all_gather x2 -> x0, waiting for transfers between devices: 102 us -> none  [the longest x1 54.2 us: on_device(): lax.all_gather(proj_out, ('blk', 'red', 'sub'), axis=0, tiled=True)]
    pallas_call x0 -> x1, Pallas kernels: none -> 63 us  [on_device_fused(): pl.pallas_call(functools.partial(fused, nz, split), out_shape=jax.ShapeDt...]
    unnamed x4 -> x0, waiting for transfers between devices: 30.1 us -> none
    dot_general x9 -> x0, matrix products: 10.6 us -> none  [the longest x1 3.58 us: on_device(): jnp.dot(masked, lax.all_gather(proj_out, ('blk', 'red', 'sub'), axis=0, t...]
    all_gather x2 -> x0, blocking collectives: 10 us -> none  [the longest x1 5.64 us: on_device(): every_coord = lax.all_gather(coords, 'red', axis=0, tiled=True)]
    reshape x3 -> x0, local copies, waits for them, and re-layouts: 4.2 us -> none  [the longest x1 4.07 us: on_device(): query_coords = queries.reshape(queries.shape[0], -1, BS)]
    all_to_all x1 -> x0, starting transfers between devices: 3.37 us -> none  [on_device(): lax.all_to_all(projected, ('blk', 'sub'), split_axis=1, concat_axis=0, ti...]
    unnamed x9 -> x8, local copies, waits for them, and re-layouts: 2.13 us -> 5.07 us
  transfers between devices with their start and end apart: 4 -> 0, of which waited for: 4 -> 0; matrix products, arithmetic and copies ran while one was open for 4% -> 0% of each run, Pallas kernels for 0% -> 0%
where the time goes in v1:
time: 69.7 us; the launch traced here: 69.5 us
  Pallas kernels  63 us (90%)
  local copies, waits for them, and re-layouts  5.07 us (7%)
    pallas_call x1, Pallas kernels, on_device_fused(): pl.pallas_call(functools.partial(fused, nz, split), out_shape=jax.ShapeDt...  63 us
    unnamed x8, local copies, waits for them, and re-layouts  5.07 us

profile of v1, /device:TPU:0, one launch (start us, length us, event | category | flops | bytes accessed | tf_op | source)
XLA Modules:
  0.0 69.5 jit_solution(17333065542814623393)
XLA Ops:
  0.7 0.0 copy-start
  0.7 1.6 %copy-done = bf16[1,1,128,8192]{3,2,1,0:T(8,128)(2,1)S(1)} copy-done((bf16[1,1,128,8192]{3,2,1,0:T(8,128)(2,1)S(1)}, bf16[1,1,128,8192]{3,2,1,0:T(8,128)(2,1)}, u32[]{:S(2)}) %copy-start) | copy-done | bytes 2097176
  2.2 0.0 copy-start.1
  2.2 1.6 %copy-done.1 = bf16[1,1,128,8192]{3,2,1,0:T(8,128)(2,1)S(1)} copy-done((bf16[1,1,128,8192]{3,2,1,0:T(8,128)(2,1)S(1)}, bf16[1,1,128,8192]{3,2,1,0:T(8,128)(2,1)}, u32[]{:S(2)}) %copy-start.1) | copy-done | bytes 2097176
  3.8 0.0 copy-start.2
  3.8 0.9 %copy-done.2 = bf16[512,256]{1,0:T(8,128)(2,1)S(1)} copy-done((bf16[512,256]{1,0:T(8,128)(2,1)S(1)}, bf16[512,256]{1,0:T(8,128)(2,1)}, u32[]{:S(2)}) %copy-start.2) | copy-done | bytes 262168
  4.8 0.0 copy-start.3
  4.8 0.9 %copy-done.3 = bf16[512,256]{1,0:T(8,128)(2,1)S(1)} copy-done((bf16[512,256]{1,0:T(8,128)(2,1)S(1)}, bf16[512,256]{1,0:T(8,128)(2,1)}, u32[]{:S(2)}) %copy-start.3) | copy-done | bytes 262168
  5.7 63.0 %shard_map.64 = f32[8,128]{1,0:T(8,128)S(1)} custom-call(bf16[128,8192]{1,0:T(8,128)(2,1)S(1)} %bitcast.4, bf16[128,8192]{1,0:T(8,128)(2,1)S(1)} %bitcast.5, s32[1,1]{1,0:T(1,128)S(6)} %copy.7.len_ref, bf16[512,256]{1,0:T(8,128)(2,1)S(1)} %copy-done.2, bf16[512,256]{1,0:T(8,128)(2,1)S(1)} %copy-done.3, bf16[128,32,256]{2,1,0:T(8,128)(2,1)} %q_hbm.1), custom_call_target="tpu_custom_call" | custom-call | flops 1073741824 | bytes 7340032 | tf_op jit(solution)/shard_map/pallas_call | solution.py:360
  68.8 0.7 multiply_bitcast_fusion
Async XLA Ops:
  0.7 1.6 %copy-start = (bf16[1,1,128,8192]{3,2,1,0:T(8,128)(2,1)S(1)}, bf16[1,1,128,8192]{3,2,1,0:T(8,128)(2,1)}, u32[]{:S(2)}) copy-start(bf16[1,1,128,8192]{3,2,1,0:T(8,128)(2,1)} %param.6) | copy-start | bytes 6291460
  2.2 1.6 %copy-start.1 = (bf16[1,1,128,8192]{3,2,1,0:T(8,128)(2,1)S(1)}, bf16[1,1,128,8192]{3,2,1,0:T(8,128)(2,1)}, u32[]{:S(2)}) copy-start(bf16[1,1,128,8192]{3,2,1,0:T(8,128)(2,1)} %param.7) | copy-start | bytes 6291460
  3.8 0.9 %copy-start.2 = (bf16[512,256]{1,0:T(8,128)(2,1)S(1)}, bf16[512,256]{1,0:T(8,128)(2,1)}, u32[]{:S(2)}) copy-start(bf16[512,256]{1,0:T(8,128)(2,1)} %pin_hbm.1) | copy-start | bytes 786436
  4.8 0.9 %copy-start.3 = (bf16[512,256]{1,0:T(8,128)(2,1)S(1)}, bf16[512,256]{1,0:T(8,128)(2,1)}, u32[]{:S(2)}) copy-start(bf16[512,256]{1,0:T(8,128)(2,1)} %pout_hbm.1) | copy-start | bytes 786436

commit v2 on v1

--- a/solution.py
+++ b/solution.py
@@ -120,17 +120,16 @@
         item.start()
 
     barrier = pltpu.get_barrier_semaphore()
-    greeted = 0
-    for dx in range(2):
-        for step in range(n_chunk):
-            if dx == 0 and step == 0:
-                continue
-            other = lax.rem(me + step, n_chunk)
-            pl.semaphore_signal(barrier, inc=1, device_id={"blk": other // 2, "red": lax.rem(x + dx, 2), "sub": lax.rem(other, 2)},
-                                device_id_type=pl.DeviceIdType.MESH)
-            greeted += 1
-    pl.semaphore_signal(barrier, inc=1, device_id={"groups": 1 - y}, device_id_type=pl.DeviceIdType.MESH)
-    pl.semaphore_wait(barrier, greeted + 1)
+
+    def greet(**device):
+        pl.semaphore_signal(barrier, inc=1, device_id=device, device_id_type=pl.DeviceIdType.MESH)
+
+    pl.when(z < nz - 1)(lambda: greet(blk=lax.min(z + 1, nz - 1)))
+    pl.when(z > 0)(lambda: greet(blk=lax.max(z - 1, 0)))
+    greet(red=1 - x)
+    greet(groups=1 - y)
+    greet(sub=1 - c)
+    pl.semaphore_wait(barrier, 3 + (z < nz - 1).astype(jnp.int32) + (z > 0).astype(jnp.int32))
 
     pending = []
 
@@ -353,8 +352,8 @@
     kb = held_rows // hh
     n_chunk = nz * 2
     n_ex = n_chunk * 2
-    split = rows * 11 // 16
-    anywhere = pl.BlockSpec(memory_space=pl.ANY)
+    split = rows * 10 // 16
+    anywhere = pl.BlockSpec(memory_space=pltpu.HBM)
     dma = pltpu.SemaphoreType.DMA
     flops = 4 * seq_len * width * rank
     total = pl.pallas_call(
@@ -383,7 +382,7 @@
             dma((n_chunk,)),
             dma((n_chunk,)),
         ],
-        compiler_params=pltpu.CompilerParams(collective_id=0, has_side_effects=True, vmem_limit_bytes=48 * 2**20),
+        compiler_params=pltpu.CompilerParams(collective_id=0, has_side_effects=True, vmem_limit_bytes=63 * 2**20),
         cost_estimate=pl.CostEstimate(flops=flops, bytes_accessed=7 * 2**20, transcendentals=0),
     )(activations.reshape(seq_len, width), out_grads.reshape(seq_len, width), lengths, proj_in, proj_out, queries)
     n_out = n_q * 2 // n_chunk

time: 69.7 us -> 61.3 us (0.88)
  local copies, waits for them, and re-layouts: 5.07 us -> 0 us
  Pallas kernels: 63 us -> 59.1 us
    unnamed x8 -> x0, local copies, waits for them, and re-layouts: 5.07 us -> none
    pallas_call x1, Pallas kernels: 63 us -> 59.1 us  [on_device_fused(): pl.pallas_call(functools.partial(fused, nz, split), out_shape=jax.ShapeDt...]
where the time goes in v2:
time: 61.3 us; the launch traced here: 61.2 us
  Pallas kernels  59.1 us (96%)
  other arithmetic  1.35 us (2%)
  between operations  0.66 us (1%)
    pallas_call x1, Pallas kernels, on_device_fused(): pl.pallas_call(functools.partial(fused, nz, split), out_shape=jax.ShapeDt...  59.1 us
    mul x1, other arithmetic, on_device_fused(): return mine.T * (1.0 / math.sqrt(BLOCKS))  1.35 us

profile of v2, /device:TPU:0, one launch (start us, length us, event | category | flops | bytes accessed | tf_op | source)
XLA Modules:
  0.0 61.2 jit_solution(2393595225696700437)
XLA Ops:
  0.7 59.1 %shard_map.64 = f32[8,128]{1,0:T(8,128)} custom-call(bf16[128,8192]{1,0:T(8,128)(2,1)} %bitcast.4, bf16[128,8192]{1,0:T(8,128)(2,1)} %bitcast.5, s32[1,1]{1,0:T(1,128)S(6)} %copy.7.len_ref, bf16[512,256]{1,0:T(8,128)(2,1)} %pin_hbm.1, bf16[512,256]{1,0:T(8,128)(2,1)} %pout_hbm.1, bf16[128,32,256]{2,1,0:T(8,128)(2,1)} %q_hbm.1), custom_call_target="tpu_custom_call" | custom-call | flops 1073741824 | bytes 7340032 | tf_op jit(solution)/shard_map/pallas_call | solution.py:359
  59.8 1.4 %multiply_bitcast_fusion = f32[32,8]{0,1:T(8,128)} fusion(f32[8,128]{1,0:T(8,128)} %shard_map.64, s32[]{:T(128)S(6)} %select_n.3), kind=kLoop, calls=%fused_computation | loop fusion | flops 256 | bytes 2052 | tf_op jit(solution)/shard_map/mul | solution.py:391

commit v3 on v2

--- a/solution.py
+++ b/solution.py
@@ -248,22 +248,27 @@
     def chunk_out(to):
         return remote(pieces.at[to], coords.at[x * n_chunk + me], asem_s.at[to], asem_r.at[me], blk=to // 2, sub=lax.rem(to, 2))
 
+    def chunk_over(to):
+        return remote(pieces.at[to], coords.at[x * n_chunk + me], xsem_s.at[to], xsem_r.at[me],
+                      blk=to // 2, red=1 - x, sub=lax.rem(to, 2))
+
     def chunk_in(frm):
         return remote(pieces.at[frm], coords.at[x * n_chunk + frm], asem_s.at[frm], asem_r.at[frm], sub=1 - c)
 
-    def across(of, side):
-        return remote(coords.at[side * n_chunk + of], coords.at[side * n_chunk + of], xsem_s.at[of], xsem_r.at[of], red=1 - x)
-
+    def over_in(frm):
+        return remote(pieces.at[frm], coords.at[(1 - x) * n_chunk + frm], xsem_s.at[frm], xsem_r.at[frm], red=1 - x)
+
+    middle = n_chunk // 2
+    for step in [middle] + [n for away in range(middle - 1, 0, -1) for n in (middle + away, middle - away)][::-1]:
+        to = lax.rem(me + step, n_chunk)
+        chunk_over(to).start()
+        chunk_out(to).start()
+    chunk_over(me).start()
+    coords[x * n_chunk + me] = pieces[me]
     for step in range(1, n_chunk):
-        chunk_out(lax.rem(me + step, n_chunk)).start()
-    coords[x * n_chunk + me] = pieces[me]
-    across(me, x).start()
-    for step in [1, 7, 2, 6, 3, 5, 4] if n_chunk == 8 else range(1, n_chunk):
-        frm = lax.rem(me + step, n_chunk)
-        chunk_in(frm).wait_recv()
-        across(frm, x).start()
-    for of in range(n_chunk):
-        across(of, 1 - x).wait_recv()
+        chunk_in(lax.rem(me + step, n_chunk)).wait_recv()
+    for frm in range(n_chunk):
+        over_in(frm).wait_recv()
 
     n_ex = coords.shape[0]
     size = n_ex * kb
@@ -334,8 +339,8 @@
             pl.when(jnp.logical_not(is_self(xx, t)))(lambda: score_out(xx, t).wait_send())
     for step in range(1, n_chunk):
         chunk_out(lax.rem(me + step, n_chunk)).wait_send()
-    for of in range(n_chunk):
-        across(of, x).wait_send()
+    for to in range(n_chunk):
+        chunk_over(to).wait_send()
     for way, p, at, when in pending:
         if when is None:
             moved(way, p, at).wait_send()

time: 61.3 us -> 60 us (0.979)
  Pallas kernels: 59.1 us -> 57.8 us
    pallas_call x1, Pallas kernels: 59.1 us -> 57.8 us  [on_device_fused(): pl.pallas_call(functools.partial(fused, nz, split), out_shape=jax.ShapeDt...]
where the time goes in v3:
time: 60 us; the launch traced here: 59.8 us
  Pallas kernels  57.8 us (96%)
  other arithmetic  1.35 us (2%)
  between operations  0.66 us (1%)
    pallas_call x1, Pallas kernels, on_device_fused(): pl.pallas_call(functools.partial(fused, nz, split), out_shape=jax.ShapeDt...  57.8 us
    mul x1, other arithmetic, on_device_fused(): return mine.T * (1.0 / math.sqrt(BLOCKS))  1.35 us

profile of v3, /device:TPU:0, one launch (start us, length us, event | category | flops | bytes accessed | tf_op | source)
XLA Modules:
  0.0 59.8 jit_solution(16188288885194344235)
XLA Ops:
  0.7 57.8 %shard_map.64 = f32[8,128]{1,0:T(8,128)} custom-call(bf16[128,8192]{1,0:T(8,128)(2,1)} %bitcast.4, bf16[128,8192]{1,0:T(8,128)(2,1)} %bitcast.5, s32[1,1]{1,0:T(1,128)S(6)} %copy.7.len_ref, bf16[512,256]{1,0:T(8,128)(2,1)} %pin_hbm.1, bf16[512,256]{1,0:T(8,128)(2,1)} %pout_hbm.1, bf16[128,32,256]{2,1,0:T(8,128)(2,1)} %q_hbm.1), custom_call_target="tpu_custom_call" | custom-call | flops 1073741824 | bytes 7340032 | tf_op jit(solution)/shard_map/pallas_call | solution.py:364
  58.5 1.4 %multiply_bitcast_fusion = f32[32,8]{0,1:T(8,128)} fusion(f32[8,128]{1,0:T(8,128)} %shard_map.64, s32[]{:T(128)S(6)} %select_n.3), kind=kLoop, calls=%fused_computation | loop fusion | flops 256 | bytes 2052 | tf_op jit(solution)/shard_map/mul | solution.py:396
